TPU v7x, 256 devices: a whole 4x4x8 slice. The times are simulated.
256 devices in a mesh: dom: 256 (over z, x, y, core).
Axes of the slice: x: 4, y: 4, z: 8, core: 2. Of those that a mesh axis runs over, the one named last changes fastest.
Arguments:
- coef_init: float32 [1024, 128], P('dom'), may hold values from -6 to 6
- basis: bfloat16 [393216, 1024], P('dom'), may hold values from -0.75 to 0.75
- basis_scale: float32 [3072], P('dom'), may hold values from 0.5 to 2
- ext_force: float32 [393216, 128], P('dom'), may hold values from -6 to 6
- precond: float32 [1024], P('dom'), may hold values from 0.5 to 6, as said below
- connectivity: int32 [115200, 8], P('dom'), may hold values from 0 to 767, as said below
- halo_nodes: int32 [65536], P('dom'), may hold values from 0 to 511, as said below
- plastic: int32 [115200], P('dom'), may hold values 0 or 1
Outputs:
- coef_final: float32 [1024, 128], P('dom')
- nodal_residual: float32 [393216, 128], P('dom')
Inputs may be any that keep to these rules, and one draw needn't show every extreme that they name: `connectivity`: each part is a structured block of 16 x 16 x 2 nodes, numbered in a part-specific order; each row lists an element's 8 corners in corner-bit order (bit 0 along x, bit 1 along y, bit 2 along z). Entries below 512 are the part's own nodes; an entry 512 + h names the node listed h-th in the next part's halo_nodes (the next part's first z layer). `halo_nodes`: the entries of one part are its own local node numbers of its first z layer, in grid order with x fastest, all distinct. `precond`: Positive.
All inputs are finite; a program needn't handle non-finite values. No bound on the sum of `plastic` on one device may be relied on, other than what follows from the above.
Results may differ from a plain program's by a relative error of at most 0.0087.
Values may be sent and summed in bfloat16 or wider, within the bound.
A program may use at most 64 MiB of HBM per device.

v0:
```python
import jax
import jax.numpy as jnp
from jax import lax
from jax.sharding import PartitionSpec as P

R = 1024
ITERS = 2
STEP_SIZE = 0.5
SHEAR_MODULUS = 1.0
LAME_FIRST = 1.5
HARDENING = 0.5
YIELD_STRESS = 3.0
EPSILON = 1e-05


def from_behind(value, axis, steps):
    count = lax.axis_size(axis)
    leading, last = (max(0, -steps), min(count, count - steps))
    return lax.ppermute(value, axis, [(source, source + steps) for source in range(leading, last)])


def corner_table():
    corner_bits = jnp.arange(8)[:, None] >> jnp.arange(3)[None, :] & 1
    return (2.0 * corner_bits.astype(jnp.float32) - 1.0) / 4.0


def element_forces(corner_disp, flags, corners):
    gradient = jnp.einsum("eaic,aj->eijc", corner_disp, corners, precision=lax.Precision.HIGHEST)
    strain = 0.5 * (gradient + jnp.swapaxes(gradient, 1, 2))
    volumetric = strain[:, 0, 0] + strain[:, 1, 1] + strain[:, 2, 2]
    identity = jnp.eye(3, dtype=jnp.float32)[None, :, :, None]
    shear_part = 2.0 * SHEAR_MODULUS * (strain - volumetric[:, None, None] / 3.0 * identity)
    magnitude = jnp.sqrt(jnp.sum(shear_part * shear_part, axis=(1, 2)))
    total_modulus = 2.0 * SHEAR_MODULUS + HARDENING
    plastic_factor = HARDENING / total_modulus + 2.0 * SHEAR_MODULUS * YIELD_STRESS / (
        total_modulus * jnp.maximum(magnitude, YIELD_STRESS)
    )
    factor = jnp.where(flags[:, None] == 1, plastic_factor, jnp.ones_like(plastic_factor))
    stress = LAME_FIRST * volumetric[:, None, None] * identity + factor[:, None, None] * shear_part
    return jnp.einsum("eijc,aj->eaic", stress, corners, precision=lax.Precision.HIGHEST)


def apply_scale(values, scales):
    return (values.reshape(scales.shape[0], -1, values.shape[-1]) * scales[:, None, None]).reshape(
        values.shape
    )


def on_device(coef_init, basis, basis_scale, ext_force, precond, connectivity, halo_nodes, plastic):
    rows_dev, cases = ext_force.shape
    node_count = rows_dev // 3
    halo_count = halo_nodes.shape[0]
    corners = corner_table()
    node_ids = jnp.arange(node_count + halo_count, dtype=jnp.int32)
    incidence = (node_ids[:, None] == connectivity.reshape(-1)[None, :]).astype(jnp.float32)
    nodal_residual = ext_force
    coef_out = coef_init
    for sweep in range(ITERS):
        lifted = jnp.dot(
            basis,
            lax.all_gather(coef_out.astype(jnp.bfloat16), "dom", axis=0, tiled=True),
            preferred_element_type=jnp.float32,
        )
        nodes = apply_scale(lifted, basis_scale).reshape(node_count, 3, cases)
        outgoing = nodes[halo_nodes]
        residual_incoming = from_behind(outgoing, "dom", -1)
        extended = jnp.concatenate([nodes, residual_incoming], axis=0)
        corner_force = element_forces(extended[connectivity], plastic, corners)
        internal = jnp.dot(
            incidence,
            corner_force.reshape(-1, 3 * cases),
            precision=lax.Precision.HIGHEST,
            preferred_element_type=jnp.float32,
        ).reshape(node_count + halo_count, 3, cases)
        returned = from_behind(internal[node_count:], "dom", 1)
        own_force = internal[:node_count].at[halo_nodes].add(returned)
        nodal_residual = ext_force - own_force.reshape(rows_dev, cases)
        scaled = apply_scale(nodal_residual, basis_scale).astype(jnp.bfloat16)
        reduced = lax.psum_scatter(
            lax.dot_general(
                basis, scaled, (((0,), (0,)), ((), ())), preferred_element_type=jnp.float32
            ),
            "dom",
            scatter_dimension=0,
            tiled=True,
        )
        update = precond[:, None] * reduced
        squares = lax.psum(jnp.sum(update * update, axis=0), "dom")
        root_mean = jnp.sqrt(squares / R + EPSILON)
        coef_out = coef_out + STEP_SIZE * update / root_mean
    return (coef_out, nodal_residual)


def solution(mesh):
    return jax.shard_map(
        on_device,
        mesh=mesh,
        in_specs=(
            P("dom", None),
            P("dom", None),
            P("dom"),
            P("dom", None),
            P("dom"),
            P("dom", None),
            P("dom"),
            P("dom"),
        ),
        out_specs=(P("dom", None), P("dom", None)),
        check_vma=False,
    )
```

profile of v0, /device:TPU:1, one launch (start us, length us, event | category | flops | bytes accessed | tf_op | source)
XLA Modules:
  0.0 1042.2 jit_solution(15831920046400500216)
XLA Ops:
  9.8 67.0 %all-gather = bf16[256,4,128]{2,1,0:T(4,128)(2,1)S(1)} all-gather(bf16[1,4,128]{2,1,0:T(4,128)(2,1)S(1)} %convert_bitcast_fusion.1), channel_id=1, replica_groups=mesh['dom'=256] {'dom'}, dimensions={0}, use_global_device_ids=true | all-gather | bytes 263168 | tf_op jit(solution)/shard_map/all_gather | solution.py:61
  83.8 3.0 gather_fusion
  92.8 4.8 collective-permute-done
  97.6 3.0 pad_maximum_fusion
  100.6 14.1 %gather_fusion.1 = f32[3600,3,128]{2,1,0:T(4,128)} fusion(f32[768,3,128]{2,1,0:T(4,128)} %pad_maximum_fusion, s32[4096]{0:T(1024)S(1)} %pad_clamp_fusion), kind=kCustom, calls=%fused_computation.1 | custom fusion | bytes 11073600 | tf_op jit(solution)/shard_map/gather | solution.py:68
  114.7 8.2 fusion.6
  127.3 4.6 multiply_add_fusion.1
  131.9 6.6 convolution_bitcast_fusion.1
  138.4 8.3 fusion.1
  158.9 26.5 %scatter_fusion = f32[512,3,128]{2,1,0:T(4,128)} fusion(f32[512,3,128]{2,1,0:T(4,128)} %copy.44, s32[256]{0:T(256)S(1)} %compare_select_fusion.1, f32[256,3,128]{2,1,0:T(4,128)} %collective-permute-done.1), kind=kCustom, calls=%fused_computation.4 | custom fusion | flops 98304 | bytes 1180672 | tf_op jit(solution)/shard_map/scatter-add | solution.py:76
  187.7 3.2 convolution_bitcast_fusion.4
  191.1 253.2 %all-reduce.5.cloned.1.call-done = f32[1024,128]{0,1:T(8,128)} async-done(((f32[1024,128]{0,1:T(8,128)}), f32[1024,128]{0,1:T(8,128)}) %all-reduce.5.cloned.1.call-update) | async-done | bytes 524304
  445.4 77.5 %psum.14 = f32[128]{0:T(128)S(1)} all-reduce(f32[128]{0:T(128)S(1)} %multiply_reduce_fusion.3), channel_id=1, replica_groups=mesh['dom'=256] {'dom'}, use_global_device_ids=true, to_apply=%region_4.5 | all-reduce | flops 128 | bytes 1024 | tf_op jit(solution)/shard_map/psum | solution.py:88
  524.4 58.8 %all-gather.1 = bf16[256,4,128]{2,1,0:T(4,128)(2,1)S(1)} all-gather(bf16[1,4,128]{2,1,0:T(4,128)(2,1)S(1)} %copy.46), channel_id=1, replica_groups=mesh['dom'=256] {'dom'}, dimensions={0}, use_global_device_ids=true | all-gather | bytes 263168 | tf_op jit(solution)/shard_map/all_gather | solution.py:61
  592.8 3.0 gather_fusion.2
  597.8 8.7 collective-permute-done.2
  609.4 14.1 %gather_fusion.3 = f32[3600,3,128]{2,1,0:T(4,128)} fusion(f32[768,3,128]{2,1,0:T(4,128)} %pad_maximum_fusion.1, s32[4096]{0:T(1024)S(1)} %pad_clamp_fusion), kind=kCustom, calls=%fused_computation.3 | custom fusion | bytes 11073600 | tf_op jit(solution)/shard_map/gather | solution.py:68
  623.5 8.2 fusion.4
  636.0 4.6 multiply_add_fusion
  640.6 6.6 convolution_bitcast_fusion
  647.2 8.3 fusion
  665.9 26.5 %scatter_fusion.1 = f32[512,3,128]{2,1,0:T(4,128)} fusion(f32[512,3,128]{2,1,0:T(4,128)} %copy.53, s32[256]{0:T(256)S(1)} %compare_select_fusion.1, f32[256,3,128]{2,1,0:T(4,128)} %collective-permute-done.3), kind=kCustom, calls=%fused_computation.5 | custom fusion | flops 98304 | bytes 1180672 | tf_op jit(solution)/shard_map/scatter-add | solution.py:76
  698.9 256.0 %all-reduce.7.cloned.1.call-done = f32[1024,128]{0,1:T(8,128)} async-done(((f32[1024,128]{0,1:T(8,128)}), f32[1024,128]{0,1:T(8,128)}) %all-reduce.7.cloned.1.call-update) | async-done | bytes 524304
  955.9 77.5 %psum.15 = f32[128]{0:T(128)S(1)} all-reduce(f32[128]{0:T(128)S(1)} %multiply_reduce_fusion.2), channel_id=1, replica_groups=mesh['dom'=256] {'dom'}, use_global_device_ids=true, to_apply=%region_9.10 | all-reduce | flops 128 | bytes 1024 | tf_op jit(solution)/shard_map/psum | solution.py:88
  (96 shorter events, 75.0 us)
Async XLA Ops:
  7.2 69.6 %copy-start = (bf16[1536,1024]{1,0:T(8,128)(2,1)S(1)}, bf16[1536,1024]{1,0:T(8,128)(2,1)}, u32[]{:S(2)}) copy-start(bf16[1536,1024]{1,0:T(8,128)(2,1)} %param.9) | copy-start | bytes 9437188
  7.2 437.2 %all-reduce.5.cloned.1.call-start = ((), (), s32[]{:S(2)}) async-start(), calls=%async_computation | async-start | bytes 1048576
  78.7 10.2 copy-start.6
  78.7 14.1 %copy-start.14 = (s32[450]{0:T(512)S(1)}, s32[450]{0:T(512)}, u32[]{:S(2)}) copy-start(s32[450]{0:T(512)} %param.15) | copy-start | bytes 5404
  86.8 10.8 %collective-permute-start = (f32[256,3,128]{2,1,0:T(4,128)}, f32[256,3,128]{2,1,0:T(4,128)}, u32[]{:S(2)}, u32[]{:S(2)}) collective-permute-start(f32[256,3,128]{2,1,0:T(4,128)} %gather_fusion), channel_id=1, source_target_pairs={{1,0},{2,1},{3,2},{4,3},{5,4},{6,5},{7,6},{8,7},{9,8},{10,9},{11,1... | collective-permute-start | bytes 1179656 | tf_op jit(solution)/shard_map/ppermute | solution.py:19
  92.7 45.7 %copy-start.7 = (s32[3600]{0:T(1024)}, s32[3600]{0:T(1024)S(1)}, u32[]{:S(2)}) copy-start(s32[3600]{0:T(1024)S(1)} %eq.35) | copy-start | bytes 43204
  138.4 14.0 %copy-start.13 = (f32[12]{0:T(128)S(1)}, f32[12]{0:T(128)}, u32[]{:S(2)}) copy-start(f32[12]{0:T(128)} %param.10) | copy-start | bytes 148
  146.8 1.0 copy-start.2
  150.5 8.3 collective-permute-start.1
  187.7 3.3 copy-start.10
  187.7 256.6 %copy-start.9 = (f32[4]{0:T(128)S(1)}, f32[4]{0:T(128)}, u32[]{:S(2)}) copy-start(f32[4]{0:T(128)} %param.12) | copy-start | bytes 52
  190.9 764.0 %all-reduce.7.cloned.1.call-start = ((), (), s32[]{:S(2)}) async-start(), calls=%async_computation.1 | async-start | bytes 1048576
  191.1 396.6 %copy-start.4 = (f32[4,128]{0,1:T(8,128)}, f32[4,128]{0,1:T(8,128)S(1)}, u32[]{:S(2)}) copy-start(f32[4,128]{0,1:T(8,128)S(1)} %copy.45) | copy-start | bytes 6148
  522.9 0.5 copy-start.11
  595.8 10.8 %collective-permute-start.2 = (f32[256,3,128]{2,1,0:T(4,128)}, f32[256,3,128]{2,1,0:T(4,128)S(1)}, u32[]{:S(2)}, u32[]{:S(2)}) collective-permute-start(f32[256,3,128]{2,1,0:T(4,128)} %gather_fusion.2), channel_id=1, source_target_pairs={{1,0},{2,1},{3,2},{4,3},{5,4},{6,5},{7,6},{8,7},{9,8},{10,9},{11,1... | collective-permute-start | bytes 1179656 | tf_op jit(solution)/shard_map/ppermute | solution.py:19
  640.6 6.6 copy-start.8
  655.5 1.0 copy-start.3
  657.5 8.3 collective-permute-start.3
  696.1 0.9 copy-start.1
  697.0 336.4 %copy-start.5 = (f32[4,128]{0,1:T(8,128)S(1)}, f32[4,128]{0,1:T(8,128)}, u32[]{:S(2)}) copy-start(f32[4,128]{0,1:T(8,128)} %copy-done.4) | copy-start | bytes 6148
  697.0 336.4 %copy-start.12 = (f32[128]{0:T(128)S(1)}, f32[128]{0:T(128)}, u32[]{:S(2)}) copy-start(f32[128]{0:T(128)} %copy-done.11) | copy-start | bytes 1540
Sparse Core Ops, SparseCore 0:
  191.0 253.2 all-reduce.4
  699.0 255.8 all-reduce.6
where the time goes:
time: 1050 us; the launch traced here: 1040 us
  waiting for transfers between devices  527 us (50%)
  blocking collectives  281 us (27%)
  other arithmetic  89.2 us (8%)
  local copies, waits for them, and re-layouts  67.7 us (6%)
  matrix products  55 us (5%)
  between operations  14.7 us (1%)
    unnamed x4, waiting for transfers between devices  509 us
    psum x2, blocking collectives, on_device(): squares = lax.psum(jnp.sum(update * update, axis=0), 'dom')  155 us
    all_gather x2, blocking collectives, on_device(): lax.all_gather(coef_out.astype(jnp.bfloat16), 'dom', axis=0, tiled=True)  126 us
    scatter-add x2, other arithmetic, on_device(): own_force = internal[:node_count].at[halo_nodes].add(returned)  53.1 us
    gather x2, local copies, waits for them, and re-layouts, on_device(): corner_force = element_forces(extended[connectivity], plastic, corners)  28.2 us
  transfers between devices with their start and end apart: 6, of which 6 were waited for; matrix products, arithmetic and copies ran while one was open for 1% of the time, Pallas kernels for 0%

commit v1 on v0

--- a/solution.py
+++ b/solution.py
@@ -1,3 +1,4 @@
+import functools
 import jax
 import jax.numpy as jnp
 from jax import lax
@@ -11,6 +12,13 @@
 HARDENING = 0.5
 YIELD_STRESS = 3.0
 EPSILON = 1e-05
+
+
+def wall_enter(inp, along_axis):
+    return jax.lax.all_gather(inp, axis_name=along_axis).sum(axis=0)
+
+
+follow_vector = functools.partial(wall_enter, along_axis="dom")
 
 
 def from_behind(value, axis, steps):
@@ -85,7 +93,7 @@
             tiled=True,
         )
         update = precond[:, None] * reduced
-        squares = lax.psum(jnp.sum(update * update, axis=0), "dom")
+        squares = follow_vector(jnp.sum(update * update, axis=0))
         root_mean = jnp.sqrt(squares / R + EPSILON)
         coef_out = coef_out + STEP_SIZE * update / root_mean
     return (coef_out, nodal_residual)

time: 1050 us -> 1020 us (0.971)
  blocking collectives: 281 us -> 245 us
    psum x2 -> x0, blocking collectives: 155 us -> none  [on_device(): squares = lax.psum(jnp.sum(update * update, axis=0), 'dom')]
    all_gather x0 -> x2, blocking collectives: none -> 118 us  [wall_enter(): return jax.lax.all_gather(inp, axis_name=along_axis).sum(axis=0)]
where the time goes in v1:
time: 1020 us; the launch traced here: 1010 us
  waiting for transfers between devices  525 us (51%)
  blocking collectives  245 us (24%)
  other arithmetic  90.7 us (9%)
  local copies, waits for them, and re-layouts  67.7 us (7%)
  matrix products  55 us (5%)
  between operations  14.7 us (1%)
    unnamed x4, waiting for transfers between devices  507 us
    all_gather x2, blocking collectives, on_device(): lax.all_gather(coef_out.astype(jnp.bfloat16), 'dom', axis=0, tiled=True)  126 us
    all_gather x2, blocking collectives, wall_enter(): return jax.lax.all_gather(inp, axis_name=along_axis).sum(axis=0)  118 us
    scatter-add x2, other arithmetic, on_device(): own_force = internal[:node_count].at[halo_nodes].add(returned)  53.1 us
    gather x2, local copies, waits for them, and re-layouts, on_device(): corner_force = element_forces(extended[connectivity], plastic, corners)  28.2 us
  transfers between devices with their start and end apart: 6, of which 6 were waited for; matrix products, arithmetic and copies ran while one was open for 1% of the time, Pallas kernels for 0%

profile of v1, /device:TPU:1, one launch (start us, length us, event | category | flops | bytes accessed | tf_op | source)
XLA Modules:
  0.0 1005.5 jit_solution(9858153377836680898)
XLA Ops:
  9.8 67.0 %all-gather.2 = bf16[256,4,128]{2,1,0:T(4,128)(2,1)S(1)} all-gather(bf16[1,4,128]{2,1,0:T(4,128)(2,1)S(1)} %convert_bitcast_fusion.1), channel_id=1, replica_groups=mesh['dom'=256] {'dom'}, dimensions={0}, use_global_device_ids=true | all-gather | bytes 263168 | tf_op jit(solution)/shard_map/all_gather | solution.py:69
  83.8 3.0 gather_fusion
  92.8 4.8 collective-permute-done
  97.6 3.0 pad_maximum_fusion
  100.6 14.1 %gather_fusion.1 = f32[3600,3,128]{2,1,0:T(4,128)} fusion(f32[768,3,128]{2,1,0:T(4,128)} %pad_maximum_fusion, s32[4096]{0:T(1024)S(1)} %pad_clamp_fusion), kind=kCustom, calls=%fused_computation.1 | custom fusion | bytes 11073600 | tf_op jit(solution)/shard_map/gather | solution.py:76
  114.7 8.2 fusion.6
  127.3 4.6 multiply_add_fusion.1
  131.9 6.6 convolution_bitcast_fusion.1
  138.4 8.3 fusion.1
  158.9 26.5 %scatter_fusion = f32[512,3,128]{2,1,0:T(4,128)} fusion(f32[512,3,128]{2,1,0:T(4,128)} %copy.44, s32[256]{0:T(256)S(1)} %compare_select_fusion.1, f32[256,3,128]{2,1,0:T(4,128)} %collective-permute-done.1), kind=kCustom, calls=%fused_computation.4 | custom fusion | flops 98304 | bytes 1180672 | tf_op jit(solution)/shard_map/scatter-add | solution.py:84
  187.7 3.2 convolution_bitcast_fusion.4
  191.1 253.2 %all-reduce.5.cloned.1.call-done = f32[1024,128]{0,1:T(8,128)} async-done(((f32[1024,128]{0,1:T(8,128)}), f32[1024,128]{0,1:T(8,128)}) %all-reduce.5.cloned.1.call-update) | async-done | bytes 524304
  445.4 61.0 %all-gather.3 = f32[256,1,128]{2,1,0:T(1,128)} all-gather(f32[1,1,128]{2,1,0:T(1,128)S(1)} %bitcast.102), channel_id=2, replica_groups=mesh['dom'=256] {'dom'}, dimensions={0}, use_global_device_ids=true | all-gather | bytes 131584 | tf_op jit(solution)/shard_map/all_gather | solution.py:18
  509.1 59.2 %all-gather.4 = bf16[256,4,128]{2,1,0:T(4,128)(2,1)S(1)} all-gather(bf16[1,4,128]{2,1,0:T(4,128)(2,1)S(1)} %copy.46), channel_id=1, replica_groups=mesh['dom'=256] {'dom'}, dimensions={0}, use_global_device_ids=true | all-gather | bytes 263168 | tf_op jit(solution)/shard_map/all_gather | solution.py:69
  577.8 3.0 gather_fusion.2
  582.9 8.6 collective-permute-done.2
  594.3 14.1 %gather_fusion.3 = f32[3600,3,128]{2,1,0:T(4,128)} fusion(f32[768,3,128]{2,1,0:T(4,128)} %pad_maximum_fusion.1, s32[4096]{0:T(1024)S(1)} %pad_clamp_fusion), kind=kCustom, calls=%fused_computation.3 | custom fusion | bytes 11073600 | tf_op jit(solution)/shard_map/gather | solution.py:76
  608.4 8.2 fusion.4
  620.9 4.6 multiply_add_fusion
  625.5 6.6 convolution_bitcast_fusion
  632.1 8.3 fusion
  650.8 26.5 %scatter_fusion.1 = f32[512,3,128]{2,1,0:T(4,128)} fusion(f32[512,3,128]{2,1,0:T(4,128)} %copy.53, s32[256]{0:T(256)S(1)} %compare_select_fusion.1, f32[256,3,128]{2,1,0:T(4,128)} %collective-permute-done.3), kind=kCustom, calls=%fused_computation.5 | custom fusion | flops 98304 | bytes 1180672 | tf_op jit(solution)/shard_map/scatter-add | solution.py:84
  683.8 254.1 %all-reduce.7.cloned.1.call-done = f32[1024,128]{0,1:T(8,128)} async-done(((f32[1024,128]{0,1:T(8,128)}), f32[1024,128]{0,1:T(8,128)}) %all-reduce.7.cloned.1.call-update) | async-done | bytes 524304
  938.9 57.5 %all-gather.5 = f32[256,1,128]{2,1,0:T(1,128)S(1)} all-gather(f32[1,1,128]{2,1,0:T(1,128)S(1)} %bitcast.103), channel_id=3, replica_groups=mesh['dom'=256] {'dom'}, dimensions={0}, use_global_device_ids=true | all-gather | bytes 131584 | tf_op jit(solution)/shard_map/all_gather | solution.py:18
  (98 shorter events, 76.5 us)
Async XLA Ops:
  7.2 69.6 %copy-start = (bf16[1536,1024]{1,0:T(8,128)(2,1)S(1)}, bf16[1536,1024]{1,0:T(8,128)(2,1)}, u32[]{:S(2)}) copy-start(bf16[1536,1024]{1,0:T(8,128)(2,1)} %param.9) | copy-start | bytes 9437188
  7.2 437.2 %all-reduce.5.cloned.1.call-start = ((), (), s32[]{:S(2)}) async-start(), calls=%async_computation | async-start | bytes 1048576
  78.7 10.2 %copy-start.6 = (s32[450,8]{0,1:T(8,128)S(1)}, s32[450,8]{0,1:T(8,128)}, u32[]{:S(2)}) copy-start(s32[450,8]{0,1:T(8,128)} %param.13) | copy-start | bytes 43204
  78.7 14.1 %copy-start.14 = (s32[450]{0:T(512)S(1)}, s32[450]{0:T(512)}, u32[]{:S(2)}) copy-start(s32[450]{0:T(512)} %param.15) | copy-start | bytes 5404
  86.8 10.8 %collective-permute-start = (f32[256,3,128]{2,1,0:T(4,128)}, f32[256,3,128]{2,1,0:T(4,128)}, u32[]{:S(2)}, u32[]{:S(2)}) collective-permute-start(f32[256,3,128]{2,1,0:T(4,128)} %gather_fusion), channel_id=1, source_target_pairs={{1,0},{2,1},{3,2},{4,3},{5,4},{6,5},{7,6},{8,7},{9,8},{10,9},{11,1... | collective-permute-start | bytes 1179656 | tf_op jit(solution)/shard_map/ppermute | solution.py:27
  92.7 45.7 %copy-start.7 = (s32[3600]{0:T(1024)}, s32[3600]{0:T(1024)S(1)}, u32[]{:S(2)}) copy-start(s32[3600]{0:T(1024)S(1)} %eq.35) | copy-start | bytes 43204
  138.4 14.0 %copy-start.13 = (f32[12]{0:T(128)S(1)}, f32[12]{0:T(128)}, u32[]{:S(2)}) copy-start(f32[12]{0:T(128)} %param.10) | copy-start | bytes 148
  146.8 1.0 copy-start.2
  150.5 8.3 collective-permute-start.1
  187.7 3.3 copy-start.10
  187.7 256.6 %copy-start.9 = (f32[4]{0:T(128)S(1)}, f32[4]{0:T(128)}, u32[]{:S(2)}) copy-start(f32[4]{0:T(128)} %param.12) | copy-start | bytes 52
  190.9 747.0 %all-reduce.7.cloned.1.call-start = ((), (), s32[]{:S(2)}) async-start(), calls=%async_computation.1 | async-start | bytes 1048576
  191.1 381.6 %copy-start.4 = (f32[4,128]{0,1:T(8,128)}, f32[4,128]{0,1:T(8,128)S(1)}, u32[]{:S(2)}) copy-start(f32[4,128]{0,1:T(8,128)S(1)} %copy.45) | copy-start | bytes 6148
  507.5 0.5 copy-start.11
  580.8 10.7 %collective-permute-start.2 = (f32[256,3,128]{2,1,0:T(4,128)}, f32[256,3,128]{2,1,0:T(4,128)S(1)}, u32[]{:S(2)}, u32[]{:S(2)}) collective-permute-start(f32[256,3,128]{2,1,0:T(4,128)} %gather_fusion.2), channel_id=1, source_target_pairs={{1,0},{2,1},{3,2},{4,3},{5,4},{6,5},{7,6},{8,7},{9,8},{10,9},{11,1... | collective-permute-start | bytes 1179656 | tf_op jit(solution)/shard_map/ppermute | solution.py:27
  625.5 6.6 copy-start.8
  640.4 1.0 copy-start.3
  642.5 8.3 collective-permute-start.3
  681.1 0.9 copy-start.1
  681.9 314.8 %copy-start.5 = (f32[4,128]{0,1:T(8,128)S(1)}, f32[4,128]{0,1:T(8,128)}, u32[]{:S(2)}) copy-start(f32[4,128]{0,1:T(8,128)} %copy-done.4) | copy-start | bytes 6148
  681.9 314.8 %copy-start.12 = (f32[128]{0:T(128)S(1)}, f32[128]{0:T(128)}, u32[]{:S(2)}) copy-start(f32[128]{0:T(128)} %copy-done.11) | copy-start | bytes 1540
Sparse Core Ops, SparseCore 0:
  191.0 253.2 all-reduce.4
  683.9 253.9 all-reduce.6
